TPU v7x, 256 devices: a whole 4x4x8 slice. The times are simulated.
256 devices in a mesh: occi: 4 (over x_hi, core), occj: 8 (over z), virt: 8 (over x_lo, y).
Axes of the slice: x: 4 (x_hi: 2, x_lo: 2; x = x_hi * 2 + x_lo), y: 4, z: 8, core: 2. Of those that a mesh axis runs over, the one named last changes fastest.
Arguments:
- amplitude: bfloat16 [80, 80, 4, 16384], P('occi', 'occj', None, 'virt'), may hold values from -6 to 6
- integral: bfloat16 [4, 16384, 2048], P('occi', 'virt'), may hold values from -0.046875 to 0.046875
- tile_mask: int32 [80, 4, 128], P('occi', None, 'virt'), may hold values 0 or 1
- pair_irrep: int32 [4, 128], P('occi', 'virt'), may hold values from 0 to 3
- slice_irrep: int32 [16], replicated, may hold values from 0 to 3
- integral_mask: int32 [4, 128, 16], P('occi', 'virt'), may hold values 0 or 1
Outputs:
- residual: bfloat16 [80, 80, 2048], P('occi', 'occj', 'virt')
All inputs are finite; a program needn't handle non-finite values. No bound on the sum of `tile_mask` or of `integral_mask` on one device may be relied on, other than what follows from the above.
Results may differ from a plain program's by a relative error of at most 0.022.
Values may be sent and summed in bfloat16 or wider, within the bound.
A program may use at most 128 MiB of HBM per device.

v0:
```python
import jax
import jax.numpy as jnp
from jax import lax
from jax.sharding import PartitionSpec as P

VB = 128


def mirrored(field):
    turned = jnp.transpose(field, (1, 0, 2))
    shape = turned.shape
    halves = turned.reshape(shape[0], shape[1], shape[2] // 2, 2)
    return halves[..., ::-1].reshape(shape)


def arrange(field, count_i, count_v):
    whole_i, rows_j, pairs = field.shape
    shaped = field.reshape(count_i, whole_i // count_i, rows_j, count_v, pairs // count_v)
    shaped = jnp.transpose(shaped, (0, 3, 1, 2, 4))
    return shaped.reshape(count_i * count_v * (whole_i // count_i), rows_j, pairs // count_v)


def shards(amplitude, integral, tile_mask, pair_irrep, slice_irrep, integral_mask):
    rows_i, rows_j, groups, width = amplitude.shape
    blocks = tile_mask.shape[2]
    col_mask = jnp.broadcast_to(tile_mask[:, :, :, None], (rows_i, groups, blocks, VB)).reshape(
        rows_i, 1, groups, width
    )
    masked = amplitude * col_mask.astype(jnp.bfloat16)
    received = lax.all_to_all(masked, "occi", split_axis=2, concat_axis=0, tiled=True)
    whole_i = received.shape[0]
    flat_rows = received.reshape(whole_i * rows_j, width)
    pairs = integral.shape[2]
    slice_blocks = slice_irrep.shape[0]
    keep = (pair_irrep[0][:, None] == slice_irrep[None, :]) * integral_mask[0]
    weights = integral[0].reshape(blocks, VB, slice_blocks, pairs // slice_blocks) * keep[
        :, None, :, None
    ].astype(jnp.bfloat16)
    effective = weights.reshape(width, pairs)
    partial_sum = jnp.dot(flat_rows, effective, preferred_element_type=jnp.float32).astype(
        jnp.bfloat16
    )
    partial_sum = partial_sum.reshape(whole_i, rows_j, pairs)
    turned = lax.all_to_all(partial_sum, "occj", split_axis=0, concat_axis=1, tiled=True)
    flipped = mirrored(turned)
    count_i = lax.axis_size("occi")
    count_v = lax.axis_size("virt")
    direct = arrange(partial_sum.astype(jnp.float32), count_i, count_v)
    across = arrange(flipped.astype(jnp.float32), count_i, count_v)
    first, second = (
        lax.psum_scatter(
            direct.astype(jnp.bfloat16), ("occi", "virt"), scatter_dimension=0, tiled=True
        ).astype(jnp.float32),
        lax.psum_scatter(
            across.astype(jnp.bfloat16), ("occi", "virt"), scatter_dimension=0, tiled=True
        ).astype(jnp.float32),
    )
    result = first + second
    return result.astype(jnp.bfloat16)


def solution(mesh):
    placed = (
        P("occi", "occj", None, "virt"),
        P("occi", "virt", None),
        P("occi", None, "virt"),
        P("occi", "virt"),
        P(),
        P("occi", "virt", None),
    )
    return jax.shard_map(
        shards, mesh=mesh, in_specs=placed, out_specs=P("occi", "occj", "virt"), check_vma=False
    )
```

profile of v0, /device:TPU:37, one launch (start us, length us, event | category | flops | bytes accessed | tf_op | source)
XLA Modules:
  0.0 480.8 jit_solution(14304691603111058513)
XLA Ops:
  6.5 0.8 convert_element_type.59
  7.3 0.1 copy.21
  7.4 0.2 broadcast_in_dim.2
  7.7 0.2 convert_element_type.60
  7.9 7.5 %copy_multiply_fusion = bf16[20,10,4,2048]{3,0,1,2:T(8,128)(2,1)} fusion(bf16[20,10,4,2048]{3,2,1,0:T(4,128)(2,1)} %param.6, bf16[20,4,2048]{2,0,1:T(8,128)(2,1)S(1)} %convert_element_type.60), kind=kLoop, calls=%fused_computation.5 | loop fusion | flops 1638400 | bytes 6881280 | tf_op jit(solution)/shard_map/mul | solution.py:29
  15.3 0.0 copy-start
  15.3 0.0 copy-start.1
  15.3 0.0 copy-start.2
  15.3 5.7 %all-to-all-start = ((bf16[20,10,4,2048]{3,0,1,2:T(8,128)(2,1)}), bf16[20,10,4,2048]{3,0,1,2:T(8,128)(2,1)}, u32[]{:S(2)}, u32[]{:S(2)}) async-start(bf16[20,10,4,2048]{3,0,1,2:T(8,128)(2,1)} %copy_multiply_fusion), calls=%async_computation | async-start | bytes 7864320 | tf_op jit(solution)/shard_map/all_to_all | solution.py:30
  21.1 0.0 copy-done
  21.1 0.0 copy-done.1
  21.1 0.0 copy-done.2
  21.1 0.1 fusion.6
  21.1 4.4 mul.28
  25.5 13.4 %mul.29 = bf16[1,2048,2048]{2,1,0:T(8,128)(2,1)} reshape(bf16[16,128,16,128]{3,2,1,0:T(8,128)(2,1)} %mul.28) | data formatting | bytes 16777216 | tf_op jit(solution)/shard_map/mul | solution.py:36
  38.9 25.7 %all-to-all-done = bf16[20,10,4,2048]{3,0,1,2:T(8,128)(2,1)} async-done(((bf16[20,10,4,2048]{3,0,1,2:T(8,128)(2,1)}), bf16[20,10,4,2048]{3,0,1,2:T(8,128)(2,1)}, u32[]{:S(2)}, u32[]{:S(2)}) %all-to-all-start) | async-done | bytes 3276832 | tf_op jit(solution)/shard_map/all_to_all | solution.py:30
  64.6 6.7 %copy.23 = bf16[4,20,10,1,2048]{4,2,1,0,3:T(8,128)(2,1)} copy(bf16[4,20,10,1,2048]{4,1,2,0,3:T(8,128)(2,1)} %bitcast.1) | data formatting | bytes 6553600 | tf_op jit(solution)/shard_map/all_to_all | solution.py:30
  71.3 6.7 %reshape.74 = bf16[800,2048]{1,0:T(8,128)(2,1)} reshape(bf16[4,20,10,1,2048]{4,2,1,0,3:T(8,128)(2,1)} %copy.23) | data formatting | bytes 6553600 | tf_op jit(solution)/shard_map/reshape | solution.py:32
  78.0 11.6 %fusion.3 = bf16[800,2048]{1,0:T(8,128)(2,1)S(1)} fusion(bf16[800,2048]{1,0:T(8,128)(2,1)} %reshape.74, bf16[1,2048,2048]{2,1,0:T(8,128)(2,1)} %param.7, bf16[1,2048,2048]{2,1,0:T(8,128)(2,1)} %mul.29), kind=kOutput, calls=%fused_computation.6 | convolution fusion | flops 6716719104 | bytes 23330816 | tf_op jit(solution)/shard_map/dot_general | solution.py:40
  89.5 3.6 reshape.75
  93.2 8.0 %all-to-all-start.1 = ((bf16[80,10,2048]{2,1,0:T(8,128)(2,1)}), bf16[80,10,2048]{2,1,0:T(8,128)(2,1)}, u32[]{:S(2)}, u32[]{:S(2)}) async-start(bf16[80,10,2048]{2,1,0:T(8,128)(2,1)} %reshape.75), calls=%async_computation.1 | async-start | bytes 10485760 | tf_op jit(solution)/shard_map/all_to_all | solution.py:44
  101.2 0.0 all-reduce.5.cloned.1.call-start
  101.2 1.1 copy.32
  102.3 3.3 copy.37
  105.6 6.2 %convert_element_type.65 = bf16[640,10,256]{2,0,1:T(8,128)(2,1)} reshape(bf16[4,8,20,10,256]{4,2,1,0,3:T(8,128)(2,1)} %bitcast.49) | data formatting | bytes 6553600 | tf_op jit(solution)/shard_map/convert_element_type | solution.py:52
  111.8 106.1 %all-to-all-done.1 = bf16[80,10,2048]{2,1,0:T(8,128)(2,1)} async-done(((bf16[80,10,2048]{2,1,0:T(8,128)(2,1)}), bf16[80,10,2048]{2,1,0:T(8,128)(2,1)}, u32[]{:S(2)}, u32[]{:S(2)}) %all-to-all-start.1) | async-done | bytes 3276832 | tf_op jit(solution)/shard_map/all_to_all | solution.py:44
  217.9 5.7 %copy.36 = bf16[8,10,10,2048]{3,2,0,1:T(8,128)(2,1)} copy(bf16[8,10,10,2048]{3,2,1,0:T(8,128)(2,1)} %bitcast.6) | data formatting | bytes 6553600 | tf_op jit(solution)/shard_map/all_to_all | solution.py:44
  223.5 5.2 %all_to_all.30 = bf16[10,80,2048]{2,1,0:T(8,128)(2,1)S(1)} reshape(bf16[10,8,10,2048]{3,2,1,0:T(8,128)(2,1)} %bitcast.47) | data formatting | bytes 6553600 | tf_op jit(solution)/shard_map/all_to_all | solution.py:44
  228.8 4.8 copy.26
  233.5 49.3 %rev.3 = bf16[80,10,1024,2]{0,3,2,1:T(2,128)(2,1)} reverse(bf16[80,10,1024,2]{0,3,2,1:T(2,128)(2,1)} %bitcast.48), dimensions={3} | reverse | bytes 6553600 | tf_op jit(solution)/shard_map/rev | solution.py:13
  282.8 29.8 %convert_element_type.67 = bf16[4,20,10,8,256]{1,0,4,3,2:T(4,128)(2,1)} reshape(bf16[80,10,1024,2]{0,3,2,1:T(2,128)(2,1)} %rev.3) | data formatting | bytes 6553600 | tf_op jit(solution)/shard_map/convert_element_type | solution.py:55
  312.6 27.2 %copy.27 = bf16[4,8,20,10,256]{4,2,1,0,3:T(8,128)(2,1)} copy(bf16[4,8,20,10,256]{2,0,4,1,3:T(4,128)(2,1)} %bitcast.46) | data formatting | bytes 6553600 | tf_op jit(solution)/shard_map/convert_element_type | solution.py:55
  339.8 6.2 %convert_element_type.69 = bf16[640,10,256]{2,0,1:T(8,128)(2,1)} reshape(bf16[4,8,20,10,256]{4,2,1,0,3:T(8,128)(2,1)} %copy.27) | data formatting | bytes 6553600 | tf_op jit(solution)/shard_map/convert_element_type | solution.py:55
  345.9 0.0 copy-start.3
  345.9 0.0 all-reduce.5.cloned.1.call-update
  346.0 0.6 copy-done.3
  346.6 0.6 dynamic-slice
  347.9 124.3 %all-reduce.5.cloned.1.call-done = (bf16[640,10,256]{2,0,1:T(8,128)(2,1)}, bf16[640,10,256]{2,0,1:T(8,128)(2,1)}) async-done(((bf16[640,10,256]{2,0,1:T(8,128)(2,1)}, bf16[640,10,256]{2,0,1:T(8,128)(2,1)}), (bf16[640,10,256]{2,0,1:T(8,128)(2,1)}, bf16[640,10,256]{2,0,1:T(8,128)(2,1)})) %all-reduce.5.cloned.1.call-update) | async-done | bytes 6553616
  472.2 1.7 add_convert_fusion
Async XLA Ops:
  15.3 5.7 %copy-start = (s32[1,16,16]{2,1,0:T(8,128)S(1)}, s32[1,16,16]{2,1,0:T(8,128)}, u32[]{:S(2)}) copy-start(s32[1,16,16]{2,1,0:T(8,128)} %param.11) | copy-start | bytes 3076
  15.3 5.7 %copy-start.1 = (s32[16]{0:T(128)S(1)}, s32[16]{0:T(128)}, u32[]{:S(2)}) copy-start(s32[16]{0:T(128)} %param.10) | copy-start | bytes 196
  15.3 5.7 %copy-start.2 = (s32[1,16]{1,0:T(1,128)S(1)}, s32[1,16]{1,0:T(1,128)}, u32[]{:S(2)}) copy-start(s32[1,16]{1,0:T(1,128)} %param.9) | copy-start | bytes 196
  15.3 49.3 %all-to-all-start = ((bf16[20,10,4,2048]{3,0,1,2:T(8,128)(2,1)}), bf16[20,10,4,2048]{3,0,1,2:T(8,128)(2,1)}, u32[]{:S(2)}, u32[]{:S(2)}) async-start(bf16[20,10,4,2048]{3,0,1,2:T(8,128)(2,1)} %copy_multiply_fusion), calls=%async_computation | async-start | bytes 7864320 | tf_op jit(solution)/shard_map/all_to_all | solution.py:30
  93.2 124.7 %all-to-all-start.1 = ((bf16[80,10,2048]{2,1,0:T(8,128)(2,1)}), bf16[80,10,2048]{2,1,0:T(8,128)(2,1)}, u32[]{:S(2)}, u32[]{:S(2)}) async-start(bf16[80,10,2048]{2,1,0:T(8,128)(2,1)} %reshape.75), calls=%async_computation.1 | async-start | bytes 10485760 | tf_op jit(solution)/shard_map/all_to_all | solution.py:44
  101.2 371.0 %all-reduce.5.cloned.1.call-start = ((), (), s32[]{:S(2)}) async-start(), calls=%async_computation.2 | async-start | bytes 13107200
  345.9 0.7 copy-start.3
Sparse Core Ops, SparseCore 0:
  346.1 126.0 all-reduce.4
where the time goes:
time: 489 us; the launch traced here: 481 us
  waiting for transfers between devices  256 us (52%)
  local copies, waits for them, and re-layouts  175 us (36%)
  between operations  14.1 us (3%)
  starting transfers between devices  13.7 us (3%)
  matrix products  11.6 us (2%)
  other arithmetic  10.1 us (2%)
    unnamed x2, waiting for transfers between devices  124 us
    all_to_all x1, waiting for transfers between devices, shards(): lax.all_to_all(partial_sum, 'occj', split_axis=0, concat_axis=1, tiled=True)  106 us
    convert_element_type x3, local copies, waits for them, and re-layouts, shards(): across.astype(jnp.bfloat16)  63.1 us
    rev x1, local copies, waits for them, and re-layouts, mirrored(): return halves[..., ::-1].reshape(shape)  49.3 us
    all_to_all x1, waiting for transfers between devices, shards(): lax.all_to_all(masked, 'occi', split_axis=2, concat_axis=0, tiled=True)  25.7 us
    mul x2, local copies, waits for them, and re-layouts, shards(): integral[0].reshape(blocks, VB, slice_blocks, pairs // slice_blocks)  17.8 us
    dot_general x1, matrix products, shards(): jnp.dot(flat_rows, effective, preferred_element_type=jnp.float32)  11.6 us
    all_to_all x2, local copies, waits for them, and re-layouts, shards(): lax.all_to_all(partial_sum, 'occj', split_axis=0, concat_axis=1, tiled=True)  10.9 us
  transfers between devices with their start and end apart: 3, of which 3 were waited for; matrix products, arithmetic and copies ran while one was open for 6% of the time, Pallas kernels for 0%

commit v1 on v0

v1 whole, which is shorter than its diff:
```python
import jax
import jax.numpy as jnp
from jax import lax
from jax.experimental import pallas as pl
from jax.experimental.pallas import tpu as pltpu
from jax.sharding import PartitionSpec as P

MESH = pl.DeviceIdType.MESH
BF = jnp.bfloat16
F32 = jnp.float32
CH = 5
CR = 40
BL = 16
VB = 128
W = BL * VB
NB = 8
NW = 256
BLK = 112


def iota(shape, axis):
    return lax.broadcasted_iota(jnp.int32, shape, axis)


def matmul(a, b):
    return jnp.dot(a, b, preferred_element_type=F32)


def kernel(
    amp, vint, tm, pi, si, im, out,
    raw, ma, lh, lhs, v, kx, wm, perm, expand, sel, turn, swap,
    pk, cs, cr, ys, yr, xt, xs, xr, total, ts, tr,
    raw_sem, v_sem, a_ss, a_rs, c_ss, c_rs, y_ss, y_rs, x_ss, x_rs, t_ss, t_rs, t_ls,
):
    occi, z, virt = lax.axis_index("occi"), lax.axis_index("occj"), lax.axis_index("virt")
    xh, c = occi // 2, occi % 2
    xl, y = virt // 4, virt % 4

    def dev(h, core, low, yy):
        return (2 * h + core, z, 4 * low + yy)

    sibling = dev(xh, 1 - c, xl, y)
    far_same = dev(1 - xh, c, xl, y)
    far_other = dev(1 - xh, 1 - c, xl, y)
    near = dev(xh, c, 1 - xl, y)
    far_near = dev(1 - xh, c, 1 - xl, y)
    y_peer = [dev(xh, c, xl, (y + d) % 4) for d in (1, 2, 3)]
    turned = [(z // 2, 2 * occi + h, virt) for h in (0, 1)]
    on_diag = (z // 2) == occi
    here = z % 2

    def raw_copy(k, t):
        return pltpu.make_async_copy(
            amp.at[pl.ds(k * CR, CR), t], raw.at[k * BL + t], raw_sem.at[k]
        )

    def start_raw(k, _):
        for t in range(BL):
            raw_copy(k, t).start()
        return 0

    def v_copy(n):
        return pltpu.make_async_copy(
            vint.at[0, :, pl.ds(pl.multiple_of(n * NW, NW), NW)], v.at[n], v_sem.at[n]
        )

    def start_v(n, _):
        v_copy(n).start()
        return 0

    lax.fori_loop(0, CH, start_raw, 0)
    lax.fori_loop(0, NB, start_v, 0)

    barrier = pltpu.get_barrier_semaphore()
    for peer in [sibling, far_same, far_other, near, far_near] + y_peer:
        pl.semaphore_signal(barrier, inc=1, device_id=peer, device_id_type=MESH)
    for h in (0, 1):
        @pl.when(jnp.logical_not(jnp.logical_and(on_diag, here == h)))
        def _():
            pl.semaphore_signal(barrier, inc=1, device_id=turned[h], device_id_type=MESH)

    row, col = iota((4 * CR, 4 * CR), 0), iota((4 * CR, 4 * CR), 1)
    perm[...] = jnp.where(col == (row % CR) * 4 + row // CR, 1.0, 0.0).astype(BF)
    expand[...] = jnp.where(iota((BL, W), 1) // VB == iota((BL, W), 0), 1.0, 0.0).astype(BF)
    ri, ci = iota((CH * CR, 20), 0), iota((CH * CR, 20), 1)
    own_i = jnp.where(ri // 10 == ci, 1.0, 0.0).astype(BF)
    for q in range(4):
        flags = lax.dot_general(
            own_i, tm[q].astype(F32).astype(BF), (((1,), (1,)), ((), ())),
            preferred_element_type=F32,
        )
        for k in range(CH):
            wm[k, q * CR:(q + 1) * CR, :] = flags[k * CR:(k + 1) * CR, :]

    def a_copies(k):
        far_q = 2 * (1 - xh)
        plan = (
            (0, far_q + c, CH + k, 0, far_same),
            (1, far_q + 1 - c, CH + k, 1, far_other),
            (2, 2 * xh + 1 - c, k, 1, sibling),
        )
        return [
            pltpu.make_async_remote_copy(
                src_ref=ma.at[q, k], dst_ref=lh.at[s, side],
                send_sem=a_ss.at[k, n], recv_sem=a_rs.at[k, n],
                device_id=peer, device_id_type=MESH,
            )
            for n, q, s, side, peer in plan
        ]

    rawf = raw.reshape(CH * BL, 4 * CR, VB)

    def spread(k, _):
        pltpu.make_async_copy(
            raw.at[pl.ds(k * BL, BL)], raw.at[pl.ds(k * BL, BL)], raw_sem.at[k]
        ).wait()
        flags = wm[k].astype(BF)
        for part in range(4):
            x = jnp.concatenate([rawf[k * BL + part * 4 + t] for t in range(4)], axis=1)
            lanes = pl.ds(part * 4 * VB, 4 * VB)
            got = matmul(perm[...], x) * matmul(flags, expand[:, lanes])
            for q in range(4):
                ma[q, k, :, lanes] = got[q * CR:(q + 1) * CR].astype(BF)

        @pl.when(k == 0)
        def _():
            pl.semaphore_wait(barrier, 10 - on_diag.astype(jnp.int32))

        for copy in a_copies(k):
            copy.start()
        lh[k, 0] = ma[2 * xh + c, k]
        return 0

    lax.fori_loop(0, CH, spread, 0)

    eye = iota((BL, BL), 0) == iota((BL, BL), 1)
    own_label = jnp.sum(jnp.where(eye, pi[...], 0), axis=1, keepdims=True)
    keep = jnp.where(own_label == si[...], im[0], 0).astype(F32).astype(BF)
    for n in range(NB):
        kx[n] = matmul(keep, expand[:, n * NW:(n + 1) * NW])

    def mask_v(n, _):
        v_copy(n).wait()
        for b in range(BL):
            line = jnp.broadcast_to(kx[n, b:b + 1, :], (16, NW)).astype(BF)
            rows = pl.ds(b * VB, VB)
            v[n, rows, :] = (v[n, rows, :].reshape(8, 16, NW) * line[None]).reshape(VB, NW)
        return 0

    lax.fori_loop(0, NB, mask_v, 0)

    rs, cs_ = iota((2 * BLK, CH * CR), 0), iota((2 * BLK, CH * CR), 1)
    part_s = rs % BLK
    sel[...] = jnp.where(
        jnp.logical_and(part_s < 100, cs_ == 100 * (rs // BLK) + part_s), 1.0, 0.0
    ).astype(BF)
    rt, ct = iota((CH * CR, 2 * BLK), 0), iota((CH * CR, 2 * BLK), 1)
    it, jt = rt // 10, rt % 10
    turn[...] = jnp.where(ct == BLK * (it // 10) + jt * 10 + it % 10, 1.0, 0.0).astype(BF)
    aw, bw = iota((NW, NW), 0), iota((NW, NW), 1)
    swap[...] = jnp.where(aw == bw + 1 - 2 * (bw % 2), 1.0, 0.0).astype(BF)

    def c_copy(s):
        return pltpu.make_async_remote_copy(
            src_ref=cs.at[s], dst_ref=cr.at[s], send_sem=c_ss.at[s], recv_sem=c_rs.at[s],
            device_id=sibling, device_id_type=MESH,
        )

    def y_copies(s):
        return [
            pltpu.make_async_remote_copy(
                src_ref=ys.at[s, :, (y + d) % 4], dst_ref=yr.at[s, d - 1],
                send_sem=y_ss.at[s, d - 1], recv_sem=y_rs.at[s, d - 1],
                device_id=y_peer[d - 1], device_id_type=MESH,
            )
            for d in (1, 2, 3)
        ]

    def x_copy(s, n, source, low, peer):
        return pltpu.make_async_remote_copy(
            src_ref=xs.at[source, low], dst_ref=xr.at[s, n],
            send_sem=x_ss.at[s, n], recv_sem=x_rs.at[s, n],
            device_id=peer, device_id_type=MESH,
        )

    def x_copies(k):
        return [
            x_copy(k, 0, k, 1 - xl, near),
            x_copy(k, 1, CH + k, xl, far_same),
            x_copy(k, 2, CH + k, 1 - xl, far_near),
        ]

    def multiply(s):
        @pl.when(s < CH)
        def _():
            a_copies(s)[2].wait_recv()

        @pl.when(s >= CH)
        def _():
            a_copies(s - CH)[0].wait_recv()
            a_copies(s - CH)[1].wait_recv()

        lhs[...] = jnp.concatenate(
            [lh[s, 0].astype(F32), lh[s, 1].astype(F32)], axis=0
        ).astype(BF)

        def column(n, _):
            got = matmul(lhs[...], v[n])
            pk[s, n // 4, n % 4] = got[:CR]
            cs[s, n // 4, n % 4] = got[CR:].astype(BF)
            return 0

        lax.fori_loop(0, NB, column, 0)
        c_copy(s).start()

    def over_cores(s):
        c_copy(s).wait_recv()
        for low in range(2):
            for yy in range(4):
                both = pk[s, low, yy] + cr[s, low, yy].astype(F32)
                pk[s, low, yy] = both
                ys[s, low, yy] = both.astype(BF)
        for copy in y_copies(s):
            copy.start()

    def over_y(s):
        for copy in y_copies(s):
            copy.wait_recv()
        for low in range(2):
            both = pk[s, low, y]
            for d in range(3):
                both = both + yr[s, d, low].astype(F32)
            xt[s, low] = both
            xs[s, low] = both.astype(BF)

        @pl.when(s < CH)
        def _():
            x_copies(s)[0].start()

        @pl.when(s >= CH)
        def _():
            x_copies(s - CH)[1].start()
            x_copies(s - CH)[2].start()

    def over_x(k):
        for copy in x_copies(k):
            copy.wait_recv()
        both = xt[k, xl]
        for d in range(3):
            both = both + xr[k, d].astype(F32)
        total[pl.ds(pl.multiple_of(k * CR, 8), CR), :] = both

    def step(s, _):
        multiply(s)
        over_cores(s)

        @pl.when(s >= 1)
        def _():
            over_y(s - 1)

        @pl.when(s >= CH + 2)
        def _():
            over_x(s - CH - 2)

        return 0

    lax.fori_loop(0, 2 * CH, step, 0)
    over_y(2 * CH - 1)
    over_x(CH - 2)
    over_x(CH - 1)

    mirrored = matmul(total[...].astype(BF), swap[...]).astype(BF)
    blocks = matmul(sel[...], mirrored).astype(BF)
    for h in (0, 1):
        ts[h] = blocks[h * BLK:(h + 1) * BLK]

    def t_copy(h):
        return pltpu.make_async_remote_copy(
            src_ref=ts.at[h], dst_ref=tr.at[here], send_sem=t_ss.at[h], recv_sem=t_rs.at[here],
            device_id=turned[h], device_id_type=MESH,
        )

    def t_arrival(h):
        return pltpu.make_async_remote_copy(
            src_ref=ts.at[h], dst_ref=tr.at[h], send_sem=t_ss.at[h], recv_sem=t_rs.at[h],
            device_id=turned[h], device_id_type=MESH,
        )

    def t_local(h):
        return pltpu.make_async_copy(ts.at[h], tr.at[h], t_ls)

    for h in (0, 1):
        mine = jnp.logical_and(on_diag, here == h)

        @pl.when(mine)
        def _():
            t_local(h).start()

        @pl.when(jnp.logical_not(mine))
        def _():
            t_copy(h).start()

    def sent(k, _):
        for copy in a_copies(k) + x_copies(k):
            copy.wait_send()
        return 0

    def sent_sums(s, _):
        for copy in [c_copy(s)] + y_copies(s):
            copy.wait_send()
        return 0

    lax.fori_loop(0, CH, sent, 0)
    lax.fori_loop(0, 2 * CH, sent_sums, 0)

    for h in (0, 1):
        mine = jnp.logical_and(on_diag, here == h)

        @pl.when(mine)
        def _():
            t_local(h).wait()

        @pl.when(jnp.logical_not(mine))
        def _():
            t_arrival(h).wait_recv()
            t_copy(h).wait_send()

    arrived = jnp.concatenate([tr[0], tr[1]], axis=0)
    out[...] = (total[...] + matmul(turn[...], arrived)).astype(BF)


def shards(amplitude, integral, tile_mask, pair_irrep, slice_irrep, integral_mask):
    rows_i, rows_j, groups, width = amplitude.shape
    rows = rows_i * rows_j
    tiles = amplitude.reshape(rows, groups, BL, VB).transpose(0, 2, 1, 3)
    steps = 2 * CH
    dma = pltpu.SemaphoreType.DMA
    vmem = pl.BlockSpec(memory_space=pltpu.VMEM)
    hbm = pl.BlockSpec(memory_space=pl.ANY)
    result = pl.pallas_call(
        kernel,
        out_shape=jax.ShapeDtypeStruct((rows, NW), BF),
        in_specs=[hbm, hbm, vmem, vmem, vmem, vmem],
        out_specs=vmem,
        scratch_shapes=[
            pltpu.VMEM((CH * BL, CR, groups, VB), BF),
            pltpu.VMEM((groups, CH, CR, W), BF),
            pltpu.VMEM((steps, 2, CR, W), BF),
            pltpu.VMEM((2 * CR, W), BF),
            pltpu.VMEM((NB, W, NW), BF),
            pltpu.VMEM((NB, BL, NW), F32),
            pltpu.VMEM((CH, groups * CR, BL), F32),
            pltpu.VMEM((groups * CR, groups * CR), BF),
            pltpu.VMEM((BL, W), BF),
            pltpu.VMEM((2 * BLK, rows), BF),
            pltpu.VMEM((rows, 2 * BLK), BF),
            pltpu.VMEM((NW, NW), BF),
            pltpu.VMEM((steps, 2, 4, CR, NW), F32),
            pltpu.VMEM((steps, 2, 4, CR, NW), BF),
            pltpu.VMEM((steps, 2, 4, CR, NW), BF),
            pltpu.VMEM((steps, 2, 4, CR, NW), BF),
            pltpu.VMEM((steps, 3, 2, CR, NW), BF),
            pltpu.VMEM((steps, 2, CR, NW), F32),
            pltpu.VMEM((steps, 2, CR, NW), BF),
            pltpu.VMEM((CH, 3, CR, NW), BF),
            pltpu.VMEM((rows, NW), F32),
            pltpu.VMEM((2, BLK, NW), BF),
            pltpu.VMEM((2, BLK, NW), BF),
            dma((CH,)), dma((NB,)),
            dma((CH, 3)), dma((CH, 3)),
            dma((steps,)), dma((steps,)),
            dma((steps, 3)), dma((steps, 3)),
            dma((CH, 3)), dma((CH, 3)),
            dma((2,)), dma((2,)), dma,
        ],
        compiler_params=pltpu.CompilerParams(
            collective_id=0, has_side_effects=True, vmem_limit_bytes=52 * 2**20
        ),
        name="ladder",
    )(
        tiles, integral, tile_mask.transpose(1, 2, 0), pair_irrep,
        slice_irrep.reshape(1, -1), integral_mask,
    )
    return result.reshape(rows_i, rows_j, NW)


def solution(mesh):
    placed = (
        P("occi", "occj", None, "virt"),
        P("occi", "virt", None),
        P("occi", None, "virt"),
        P("occi", "virt"),
        P(),
        P("occi", "virt", None),
    )
    return jax.shard_map(
        shards, mesh=mesh, in_specs=placed, out_specs=P("occi", "occj", "virt"), check_vma=False
    )
```

time: 489 us -> 77.1 us (0.16); the launches traced: 481 us -> 76.9 us
  waiting for transfers between devices: 256 us -> 0 us
  local copies, waits for them, and re-layouts: 175 us -> 3.49 us
  Pallas kernels: 0 us -> 73.4 us
  between operations: 14.1 us -> 0.02 us
  starting transfers between devices: 13.7 us -> 0 us
  matrix products: 11.6 us -> 0 us
  other arithmetic: 10.1 us -> 0 us
    all_to_all x2 -> x0, waiting for transfers between devices: 132 us -> none  [the longest x1 106 us: shards(): lax.all_to_all(partial_sum, 'occj', split_axis=0, concat_axis=1, tiled=True)]
    unnamed x2 -> x0, waiting for transfers between devices: 124 us -> none
    pallas_call x0 -> x1, Pallas kernels: none -> 73.4 us  [shards(): pl.pallas_call(kernel, out_shape=jax.ShapeDtypeStruct((rows, NW), BF), in...]
    convert_element_type x7 -> x0, local copies, waits for them, and re-layouts: 72.9 us -> none  [the longest x3 63.1 us: shards(): across.astype(jnp.bfloat16)]
    rev x1 -> x0, local copies, waits for them, and re-layouts: 49.3 us -> none  [mirrored(): return halves[..., ::-1].reshape(shape)]
    mul x2 -> x0, local copies, waits for them, and re-layouts: 17.8 us -> none  [shards(): integral[0].reshape(blocks, VB, slice_blocks, pairs // slice_blocks)]
    all_to_all x3 -> x0, local copies, waits for them, and re-layouts: 17.5 us -> none  [the longest x2 10.9 us: shards(): lax.all_to_all(partial_sum, 'occj', split_axis=0, concat_axis=1, tiled=True)]
    all_to_all x2 -> x0, starting transfers between devices: 13.7 us -> none  [the longest x1 8.01 us: shards(): lax.all_to_all(partial_sum, 'occj', split_axis=0, concat_axis=1, tiled=True)]
  transfers between devices with their start and end apart: 3 -> 0, of which waited for: 3 -> 0; matrix products, arithmetic and copies ran while one was open for 6% -> 0% of each run, Pallas kernels for 0% -> 0%
where the time goes in v1:
time: 77.1 us; the launch traced here: 76.9 us
  Pallas kernels  73.4 us (95%)
  local copies, waits for them, and re-layouts  3.49 us (5%)
    pallas_call x1, Pallas kernels, shards(): pl.pallas_call(kernel, out_shape=jax.ShapeDtypeStruct((rows, NW), BF), in...  73.4 us
    unnamed x8, local copies, waits for them, and re-layouts  2.76 us

profile of v1, /device:TPU:37, one launch (start us, length us, event | category | flops | bytes accessed | tf_op | source)
XLA Modules:
  0.0 76.9 jit_solution(6281844155513306630)
XLA Ops:
  0.0 0.0 copy-start
  0.0 0.8 copy-done
  0.8 0.0 copy-start.1
  0.8 0.7 copy-done.1
  1.5 0.0 copy-start.2
  1.5 0.7 copy-done.2
  2.1 0.0 copy-start.3
  2.1 0.7 copy-done.3
  2.8 73.4 %ladder.1 = bf16[200,256]{1,0:T(8,128)(2,1)S(1)} custom-call(bf16[200,16,4,128]{3,2,1,0:T(4,128)(2,1)} %bitcast.7, bf16[1,2048,2048]{2,1,0:T(8,128)(2,1)} %vint.1, s32[4,16,20]{2,1,0:T(8,128)S(1)} %bitcast.5, s32[1,16]{1,0:T(1,128)S(1)} %copy-done.2, s32[1,16]{1,0:T(1,128)S(1)} %bitcast.6, s32[1,16,16]{2,1,0:T(8,128)S(1)} %copy-done.1), custom_call_target="tpu_custom_call" | custom-call | tf_op jit(solution)/shard_map/ladder/pallas_call | solution.py:340
  76.2 0.7 copy.8
  (1 shorter events, 0.0 us)
Async XLA Ops:
  0.0 0.8 copy-start
  0.8 0.7 copy-start.1
  1.5 0.7 copy-start.2
  2.1 0.7 copy-start.3

commit v2 on v0

v2 whole, which is shorter than its diff:
```python
import jax
import jax.numpy as jnp
from jax import lax
from jax.experimental import pallas as pl
from jax.experimental.pallas import tpu as pltpu
from jax.sharding import PartitionSpec as P

MESH = pl.DeviceIdType.MESH
BF = jnp.bfloat16
F32 = jnp.float32
ROWS = 200
SIZES = (16, 64, 64, 40, 16)
HALVES = (1, 1, 1, 1, 2)
STARTS = tuple(sum(SIZES[:k]) for k in range(len(SIZES)))
CHUNKS = range(len(SIZES))
GROUPS = ((), (0, 1), (2,), (3,), (4,))
LAST = len(GROUPS) - 1
BL = 16
VB = 128
W = BL * VB
NB = 8
NW = 256
TR = 208
TB = 112
TCUT = 96
PIECES = ((0, 0, TB), (1, TCUT, 48), (1, 144, 64))


def group_rows(g):
    return ROWS if g == 0 else sum(SIZES[k] for k in GROUPS[g])


def iota(shape, axis):
    return lax.broadcasted_iota(jnp.int32, shape, axis)


def matmul(a, b):
    return jnp.dot(a, b, preferred_element_type=F32)


def bits(condition):
    return jnp.where(condition, 1.0, 0.0).astype(BF)


def tenth(x):
    return lax.shift_right_logical(x * 205, 11)


def scratch():
    dma = pltpu.SemaphoreType.DMA
    out = dict(
        tm=pltpu.VMEM((4, BL, 20), jnp.int32),
        pi=pltpu.VMEM((1, BL), jnp.int32),
        si=pltpu.VMEM((1, BL), jnp.int32),
        im=pltpu.VMEM((1, BL, BL), jnp.int32),
        v=pltpu.VMEM((NB, W, NW), BF),
        kx=pltpu.VMEM((NB, BL, NW), F32),
        expand=pltpu.VMEM((BL, W), BF),
        turn=pltpu.VMEM((ROWS, 2 * TB), BF),
        swap=pltpu.VMEM((NW, NW), BF),
        total=pltpu.VMEM((ROWS, NW), F32),
        final=pltpu.VMEM((NW // VB, ROWS, VB), F32),
        ts=pltpu.VMEM((TR, NW), BF),
        tr=pltpu.VMEM((2, TR, NW), BF),
        small_sem=dma((4,)), v_sem=dma((NB,)),
        t_ss=dma((3,)), t_rs=dma((3, 2)), t_ls=dma((3,)),
        part=pltpu.VMEM((NB, 2 * SIZES[-1], NW), F32),
        ds=pltpu.VMEM((2, 2, 4, SIZES[-1], NW), BF),
        dr=pltpu.VMEM((2, 2, 4, SIZES[-1], NW), BF),
        d_ss=dma((2, 2, 4)), d_rs=dma((2, 2, 4)),
    )
    for k in CHUNKS:
        r = SIZES[k]
        out.update({
            f"raw{k}": pltpu.VMEM((BL, r, 4, VB), BF),
            f"ma{k}": pltpu.VMEM((4, HALVES[k], r, W // HALVES[k]), BF),
            f"got{k}": pltpu.VMEM((3, HALVES[k], r, W // HALVES[k]), BF),
            f"raw_sem{k}": dma, f"a_ss{k}": dma((3, 2)), f"a_rs{k}": dma((3, 2)),
        })
    for g in range(LAST + 1):
        r = group_rows(g)
        out[f"lhs{g}"] = pltpu.VMEM((2 * r, W), BF)
        if g == LAST:
            break
        out.update({
            f"pk{g}": pltpu.VMEM((2, 4, r, NW), F32),
            f"cs{g}": pltpu.VMEM((2, 4, r, NW), BF),
            f"cr{g}": pltpu.VMEM((2, 4, r, NW), BF),
            f"ys{g}": pltpu.VMEM((2, 4, r, NW), BF),
            f"yr{g}": pltpu.VMEM((3, 2, r, NW), BF),
            f"xt{g}": pltpu.VMEM((2, r, NW), F32),
            f"xs{g}": pltpu.VMEM((2, r, NW), BF),
            f"xr{g}": pltpu.VMEM((2, r, NW), BF),
            f"c_ss{g}": dma, f"c_rs{g}": dma,
            f"y_ss{g}": dma((3,)), f"y_rs{g}": dma((3,)),
            f"x_ss{g}": dma((2,)), f"x_rs{g}": dma((2,)),
        })
    return out


SCRATCH = scratch()


def kernel(amp, vint, tm_in, pi_in, si_in, im_in, out, *refs):
    m = dict(zip(SCRATCH, refs))
    occi, z, virt = lax.axis_index("occi"), lax.axis_index("occj"), lax.axis_index("virt")
    xh, c = occi // 2, occi % 2
    xl, y = virt // 4, virt % 4

    def dev(h, core, low, yy):
        return (2 * h + core, z, 4 * low + yy)

    sibling = dev(xh, 1 - c, xl, y)
    far_same = dev(1 - xh, c, xl, y)
    far_other = dev(1 - xh, 1 - c, xl, y)
    near = dev(xh, c, 1 - xl, y)
    far_near = dev(1 - xh, c, 1 - xl, y)
    y_peer = [dev(xh, c, xl, (y + d) % 4) for d in (1, 2, 3)]
    turned = [(z // 2, 2 * occi + h, virt) for h in (0, 1)]
    on_diag = (z // 2) == occi
    here = z % 2

    def remote(src, dst, send, recv, peer):
        return pltpu.make_async_remote_copy(
            src_ref=src, dst_ref=dst, send_sem=send, recv_sem=recv,
            device_id=peer, device_id_type=MESH,
        )

    smalls = [
        (ref, m[name], m["small_sem"].at[n])
        for n, (ref, name) in enumerate(
            ((tm_in, "tm"), (pi_in, "pi"), (si_in, "si"), (im_in, "im"))
        )
    ]

    def start_raw(k):
        def start(t, _):
            pltpu.make_async_copy(
                amp.at[pl.ds(STARTS[k], SIZES[k]), t], m[f"raw{k}"].at[t], m[f"raw_sem{k}"]
            ).start()
            return 0

        lax.fori_loop(0, BL, start, 0)

    def v_copy(n):
        return pltpu.make_async_copy(
            vint.at[0, :, pl.ds(pl.multiple_of(n * NW, NW), NW)], m["v"].at[n], m["v_sem"].at[n]
        )

    def start_v(n, _):
        v_copy(n).start()
        return 0

    pltpu.make_async_copy(*smalls[0]).start()
    start_raw(0)

    barrier = pltpu.get_barrier_semaphore()
    far = [dev(1 - xh, core, low, yy) for core in (0, 1) for low in (0, 1) for yy in range(4)]
    for peer in far + [sibling, near] + y_peer:
        pl.semaphore_signal(barrier, inc=1, device_id=peer, device_id_type=MESH)
    for h in (0, 1):
        @pl.when(jnp.logical_not(jnp.logical_and(on_diag, here == h)))
        def _():
            pl.semaphore_signal(barrier, inc=1, device_id=turned[h], device_id_type=MESH)

    start_raw(1)
    for args in smalls[1:]:
        pltpu.make_async_copy(*args).start()

    expand = m["expand"]
    expand[...] = bits(lax.shift_right_logical(iota((BL, W), 1), 7) == iota((BL, W), 0))
    pltpu.make_async_copy(*smalls[0]).wait()
    marks = [m["tm"][q].astype(F32).astype(BF) for q in range(4)]

    def a_copies(k):
        far_q = 2 * (1 - xh)
        plan = ((far_q + c, far_same), (far_q + 1 - c, far_other), (2 * xh + 1 - c, sibling))
        return [
            [
                remote(
                    m[f"ma{k}"].at[q, cut], m[f"got{k}"].at[n, cut],
                    m[f"a_ss{k}"].at[n, cut], m[f"a_rs{k}"].at[n, cut], peer,
                )
                for cut in range(HALVES[k])
            ]
            for n, (q, peer) in enumerate(plan)
        ]

    def spread(k):
        r, ma = SIZES[k], m[f"ma{k}"]
        order = jnp.concatenate(
            [bits(iota((r, 4 * r), 1) == 4 * iota((r, 4 * r), 0) + q) for q in range(4)], axis=0
        )
        gap = iota((r, 20), 0) + STARTS[k] - 10 * iota((r, 20), 1)
        own_i = bits(jnp.logical_and(gap >= 0, gap < 10))
        flags = jnp.concatenate(
            [
                lax.dot_general(own_i, mark, (((1,), (1,)), ((), ())), preferred_element_type=F32)
                for mark in marks
            ],
            axis=0,
        ).astype(BF)
        pltpu.make_async_copy(m[f"raw{k}"], m[f"raw{k}"], m[f"raw_sem{k}"]).wait()
        flat = m[f"raw{k}"].reshape(BL, 4 * r, VB)

        per_cut = 4 // HALVES[k]

        def part(p, _):
            x = jnp.concatenate([flat[p * 4 + t] for t in range(4)], axis=1)
            lanes = pl.ds(pl.multiple_of(p * 4 * VB, 4 * VB), 4 * VB)
            got = matmul(order, x) * matmul(flags, expand[:, lanes])
            into = pl.ds(pl.multiple_of(p % per_cut * 4 * VB, 4 * VB), 4 * VB)
            for q in range(4):
                ma[q, p // per_cut, :, into] = got[q * r:(q + 1) * r].astype(BF)
            return 0

        lax.fori_loop(0, 4, part, 0, unroll=4 if k == 0 else 1)

    for k in CHUNKS:
        spread(k)
        if k == 0:
            pl.semaphore_wait(barrier, 23 - on_diag.astype(jnp.int32))
        plan = a_copies(k)
        for cut in range(HALVES[k]):
            for n in range(3):
                plan[n][cut].start()
        if k + 2 in CHUNKS:
            start_raw(k + 2)
        if k == 1:
            lax.fori_loop(0, NB, start_v, 0)

    v = m["v"]
    for args in smalls[1:]:
        pltpu.make_async_copy(*args).wait()
    eye = iota((BL, BL), 0) == iota((BL, BL), 1)
    own_label = jnp.sum(jnp.where(eye, m["pi"][...], 0), axis=1, keepdims=True)
    keep = jnp.where(own_label == m["si"][...], m["im"][0], 0).astype(F32).astype(BF)
    for n in range(NB):
        m["kx"][n] = matmul(keep, expand[:, n * NW:(n + 1) * NW])

    def mask_v(n, _):
        v_copy(n).wait()
        for b in range(BL):
            line = jnp.broadcast_to(m["kx"][n, b:b + 1, :], (16, NW)).astype(BF)
            rows = pl.ds(b * VB, VB)
            v[n, rows, :] = (v[n, rows, :].reshape(8, 16, NW) * line[None]).reshape(VB, NW)
        return 0

    lax.fori_loop(0, NB, mask_v, 0)

    def c_copy(g):
        return remote(m[f"cs{g}"], m[f"cr{g}"], m[f"c_ss{g}"], m[f"c_rs{g}"], sibling)

    def y_copies(g):
        return [
            remote(
                m[f"ys{g}"].at[:, (y + d) % 4], m[f"yr{g}"].at[d - 1],
                m[f"y_ss{g}"].at[d - 1], m[f"y_rs{g}"].at[d - 1], y_peer[d - 1],
            )
            for d in (1, 2, 3)
        ]

    def x_copies(g):
        plan = ((1 - xl, near),) if g == 0 else ((xl, far_same), (1 - xl, far_near))
        return [
            remote(
                m[f"xs{g}"].at[low], m[f"xr{g}"].at[n],
                m[f"x_ss{g}"].at[n], m[f"x_rs{g}"].at[n], peer,
            )
            for n, (low, peer) in enumerate(plan)
        ]

    def stack(pieces):
        if all(piece.shape[0] % 16 == 0 for piece in pieces):
            return jnp.concatenate(pieces, axis=0)
        return jnp.concatenate([p.astype(F32) for p in pieces], axis=0).astype(BF)

    def multiply(g):
        lhs, r = m[f"lhs{g}"], group_rows(g)
        if g == 0:
            pieces = []
            for k in CHUNKS:
                for copy in a_copies(k)[2]:
                    copy.wait_recv()
            for name, slot in (("ma", 2 * xh + c), ("got", 2)):
                for k in CHUNKS:
                    cuts = [m[f"{name}{k}"][slot, cut] for cut in range(HALVES[k])]
                    pieces.append(jnp.concatenate(cuts, axis=1))
            lhs[...] = stack(pieces)
        else:
            for k in GROUPS[g]:
                for n in range(2):
                    a_copies(k)[n][0].wait_recv()
            pieces = [m[f"got{k}"][n, 0] for n in range(2) for k in GROUPS[g]]
            lhs[:, :pieces[0].shape[1]] = stack(pieces)

        def column(n, _):
            got = matmul(lhs[...], v[n])
            m[f"pk{g}"][n // 4, n % 4] = got[:r]
            m[f"cs{g}"][n // 4, n % 4] = got[r:].astype(BF)
            return 0

        half = W // 2

        def first_half(n, _):
            m["part"][n] = matmul(lhs[:, :half], v[n, :half, :])
            return 0

        def second_half(n, _):
            got = m["part"][n] + matmul(lhs[:, half:], v[n, half:, :])
            for a in range(2):
                m["ds"][a, n // 4, n % 4] = got[a * r:(a + 1) * r].astype(BF)
            return 0

        if g == LAST:
            lax.fori_loop(0, NB, first_half, 0, unroll=2)
            last = GROUPS[g][0]
            for n in range(2):
                a_copies(last)[n][1].wait_recv()
            lhs[:, half:] = stack([m[f"got{last}"][n, 1] for n in range(2)])
            lax.fori_loop(0, NB, second_half, 0, unroll=2)
        else:
            lax.fori_loop(0, NB, column, 0, unroll=1 if g == 0 else 2)
        for copy in direct() if g == LAST else [c_copy(g)]:
            copy.start()

    def over_cores(g):
        pk, cr, ys = m[f"pk{g}"], m[f"cr{g}"], m[f"ys{g}"]
        c_copy(g).wait_recv()
        for low in range(2):
            for yy in range(4):
                both = pk[low, yy] + cr[low, yy].astype(F32)
                pk[low, yy] = both
                ys[low, yy] = both.astype(BF)
        for copy in y_copies(g):
            copy.start()

    def over_y(g):
        pk, yr, xt, xs = m[f"pk{g}"], m[f"yr{g}"], m[f"xt{g}"], m[f"xs{g}"]
        for copy in y_copies(g):
            copy.wait_recv()
        for low in range(2):
            both = pk[low, y]
            for d in range(3):
                both = both + yr[d, low].astype(F32)
            xt[low] = both
            xs[low] = both.astype(BF)
        for copy in x_copies(g):
            copy.start()

    def direct():
        return [
            remote(
                m["ds"].at[a, (xl + b) % 2, (y + d) % 4], m["dr"].at[a, b, d],
                m["d_ss"].at[a, b, d], m["d_rs"].at[a, b, d],
                dev(1 - xh, (c + a) % 2, (xl + b) % 2, (y + d) % 4),
            )
            for a in range(2) for b in range(2) for d in range(4)
        ]

    total = m["total"]

    def over_x(g):
        if g == 0:
            x_copies(g)[0].wait_recv()
            total[...] = m["xt0"][xl] + m["xr0"][0].astype(F32)
            return
        first = STARTS[GROUPS[g][0]]
        rows = slice(first, first + group_rows(g))
        if g == LAST:
            for copy in direct():
                copy.wait_recv()
            terms = [m["dr"][a, b, d] for a in range(2) for b in range(2) for d in range(4)]
        else:
            for copy in x_copies(g):
                copy.wait_recv()
            terms = [m[f"xr{g}"][n] for n in range(2)]
        both = total[rows]
        for term in terms:
            both = both + term.astype(F32)
        total[rows] = both

    ts, tr = m["ts"], m["tr"]

    def t_copy(p, slot):
        h, first, rows = PIECES[p]
        return remote(
            ts.at[pl.ds(first, rows)], tr.at[slot, pl.ds(first, rows)],
            m["t_ss"].at[p], m["t_rs"].at[p, slot], turned[h],
        )

    def t_local(p):
        h, first, rows = PIECES[p]
        return pltpu.make_async_copy(
            ts.at[pl.ds(first, rows)], tr.at[h, pl.ds(first, rows)], m["t_ls"].at[p]
        )

    def t_mine(p):
        return jnp.logical_and(on_diag, here == PIECES[p][0])

    def mirror(first, rows):
        some = matmul(total[first:first + rows].astype(BF), m["swap"][...]).astype(BF)
        ts[first:first + rows, :] = some

    def t_start(p):
        @pl.when(t_mine(p))
        def _():
            t_local(p).start()

        @pl.when(jnp.logical_not(t_mine(p)))
        def _():
            t_copy(p, here).start()

    def t_wait(p):
        block = PIECES[p][0]

        @pl.when(t_mine(p))
        def _():
            t_local(p).wait()

        @pl.when(jnp.logical_not(t_mine(p)))
        def _():
            t_copy(p, here).wait_send()

        for slot in (0, 1):
            there = jnp.logical_not(jnp.logical_and(on_diag, here == slot))

            @pl.when(jnp.logical_and(here == block, there))
            def _():
                t_copy(p, slot).wait_recv()

    def matrices():
        rt, ct = iota((ROWS, 2 * TB), 0), iota((ROWS, 2 * TB), 1)
        it = tenth(rt)
        jt = rt - 10 * it
        ht = jnp.where(it >= 10, 1, 0)
        m["turn"][...] = bits(ct == TB * ht + 4 * here + jt * 10 + it - 10 * ht)
        aw, bw = iota((NW, NW), 0), iota((NW, NW), 1)
        m["swap"][...] = bits(aw == bw + 1 - 2 * jnp.bitwise_and(bw, 1))
        ts[ROWS - 8:TR, :] = jnp.zeros((16, NW), BF)

    multiply(0)
    matrices()
    over_cores(0)
    multiply(1)
    over_cores(1)
    over_y(0)
    multiply(2)
    over_y(1)
    over_cores(2)
    multiply(3)
    over_cores(3)
    over_y(2)
    multiply(4)
    over_y(3)
    over_x(0)
    over_x(1)
    over_x(2)
    mirror(0, 144)
    t_start(0)
    t_start(1)
    over_x(3)
    over_x(4)
    mirror(144, 56)
    t_start(2)

    for k in CHUNKS:
        for copies in a_copies(k):
            for copy in copies:
                copy.wait_send()
    for g in range(LAST):
        for copy in [c_copy(g)] + y_copies(g) + x_copies(g):
            copy.wait_send()
    for copy in direct():
        copy.wait_send()
    for p in range(len(PIECES)):
        t_wait(p)

    rows = pl.ds(pl.multiple_of(TCUT * here, 16), TB)
    arrived = jnp.concatenate([tr[0, rows, :], tr[1, rows, :]], axis=0)
    both = total[...] + matmul(m["turn"][...], arrived)
    for n in range(NW // VB):
        lanes = slice(n * VB, (n + 1) * VB)
        m["final"][n] = both[:, lanes]
        for j in range(10):
            out[j, :, lanes] = m["final"][n, pl.ds(j, 20, stride=10), :].astype(BF)


def shards(amplitude, integral, tile_mask, pair_irrep, slice_irrep, integral_mask):
    rows_i, rows_j, groups, _ = amplitude.shape
    tiles = amplitude.reshape(ROWS, groups, BL, VB).transpose(0, 2, 1, 3)
    hbm = pl.BlockSpec(memory_space=pltpu.HBM)
    result = pl.pallas_call(
        kernel,
        out_shape=jax.ShapeDtypeStruct((rows_j, rows_i, NW), BF),
        in_specs=[hbm] * 6,
        out_specs=pl.BlockSpec(memory_space=pltpu.VMEM),
        scratch_shapes=list(SCRATCH.values()),
        compiler_params=pltpu.CompilerParams(
            collective_id=0, has_side_effects=True, vmem_limit_bytes=56 * 2**20
        ),
        name="ladder",
    )(
        tiles, integral, tile_mask.transpose(1, 2, 0), pair_irrep,
        slice_irrep.reshape(1, -1), integral_mask,
    )
    return result.transpose(1, 0, 2)


def solution(mesh):
    placed = (
        P("occi", "occj", None, "virt"),
        P("occi", "virt", None),
        P("occi", None, "virt"),
        P("occi", "virt"),
        P(),
        P("occi", "virt", None),
    )
    return jax.shard_map(
        shards, mesh=mesh, in_specs=placed, out_specs=P("occi", "occj", "virt"), check_vma=False
    )
```

time: 489 us -> 66.9 us (0.14); the launches traced: 481 us -> 66.6 us
  waiting for transfers between devices: 256 us -> 0 us
  local copies, waits for them, and re-layouts: 175 us -> 1.56 us
  Pallas kernels: 0 us -> 65.1 us
  between operations: 14.1 us -> 0.01 us
  starting transfers between devices: 13.7 us -> 0 us
  matrix products: 11.6 us -> 0 us
  other arithmetic: 10.1 us -> 0 us
    all_to_all x2 -> x0, waiting for transfers between devices: 132 us -> none  [the longest x1 106 us: shards(): lax.all_to_all(partial_sum, 'occj', split_axis=0, concat_axis=1, tiled=True)]
    unnamed x2 -> x0, waiting for transfers between devices: 124 us -> none
    convert_element_type x7 -> x0, local copies, waits for them, and re-layouts: 72.9 us -> none  [the longest x3 63.1 us: shards(): across.astype(jnp.bfloat16)]
    pallas_call x0 -> x1, Pallas kernels: none -> 65.1 us  [shards(): pl.pallas_call(kernel, out_shape=jax.ShapeDtypeStruct((rows_j, rows_i, NW...]
    rev x1 -> x0, local copies, waits for them, and re-layouts: 49.3 us -> none  [mirrored(): return halves[..., ::-1].reshape(shape)]
    mul x2 -> x0, local copies, waits for them, and re-layouts: 17.8 us -> none  [shards(): integral[0].reshape(blocks, VB, slice_blocks, pairs // slice_blocks)]
    all_to_all x3 -> x0, local copies, waits for them, and re-layouts: 17.5 us -> none  [the longest x2 10.9 us: shards(): lax.all_to_all(partial_sum, 'occj', split_axis=0, concat_axis=1, tiled=True)]
    all_to_all x2 -> x0, starting transfers between devices: 13.7 us -> none  [the longest x1 8.01 us: shards(): lax.all_to_all(partial_sum, 'occj', split_axis=0, concat_axis=1, tiled=True)]
  transfers between devices with their start and end apart: 3 -> 0, of which waited for: 3 -> 0; matrix products, arithmetic and copies ran while one was open for 6% -> 0% of each run, Pallas kernels for 0% -> 0%
where the time goes in v2:
time: 66.9 us; the launch traced here: 66.6 us
  Pallas kernels  65.1 us (97%)
  local copies, waits for them, and re-layouts  1.56 us (2%)
    pallas_call x1, Pallas kernels, shards(): pl.pallas_call(kernel, out_shape=jax.ShapeDtypeStruct((rows_j, rows_i, NW...  65.1 us
    unnamed x1, local copies, waits for them, and re-layouts  1.56 us

profile of v2, /device:TPU:37, one launch (start us, length us, event | category | flops | bytes accessed | tf_op | source)
XLA Modules:
  0.0 66.6 jit_solution(5110287754136676438)
XLA Ops:
  0.0 65.1 %ladder.1 = bf16[10,20,256]{2,1,0:T(8,128)(2,1)} custom-call(bf16[200,16,4,128]{3,2,1,0:T(4,128)(2,1)} %bitcast.6, bf16[1,2048,2048]{2,1,0:T(8,128)(2,1)} %vint.1, s32[4,16,20]{2,1,0:T(8,128)} %bitcast.8, s32[1,16]{1,0:T(1,128)} %pi_in.1, s32[1,16]{1,0:T(1,128)} %bitcast.9, s32[1,16,16]{2,1,0:T(8,128)} %im_in.1), custom_call_target="tpu_custom_call" | custom-call | tf_op jit(solution)/shard_map/ladder/pallas_call | solution.py:493
  65.1 1.6 %copy.8 = bf16[20,10,256]{2,0,1:T(8,128)(2,1)} copy(bf16[20,10,256]{2,0,1:T(8,128)(2,1)} %bitcast.7) | data formatting | bytes 204800

commit v3 on v2

--- a/solution.py
+++ b/solution.py
@@ -14,7 +14,7 @@
 STARTS = tuple(sum(SIZES[:k]) for k in range(len(SIZES)))
 CHUNKS = range(len(SIZES))
 GROUPS = ((), (0, 1), (2,), (3,), (4,))
-LAST = len(GROUPS) - 1
+DIRECT = (3, 4)
 BL = 16
 VB = 128
 W = BL * VB
@@ -24,6 +24,7 @@
 TB = 112
 TCUT = 96
 PIECES = ((0, 0, TB), (1, TCUT, 48), (1, 144, 64))
+FROM_BOTH = tuple(k for g in DIRECT for k in GROUPS[g])
 
 
 def group_rows(g):
@@ -64,10 +65,8 @@
         tr=pltpu.VMEM((2, TR, NW), BF),
         small_sem=dma((4,)), v_sem=dma((NB,)),
         t_ss=dma((3,)), t_rs=dma((3, 2)), t_ls=dma((3,)),
-        part=pltpu.VMEM((NB, 2 * SIZES[-1], NW), F32),
-        ds=pltpu.VMEM((2, 2, 4, SIZES[-1], NW), BF),
-        dr=pltpu.VMEM((2, 2, 4, SIZES[-1], NW), BF),
-        d_ss=dma((2, 2, 4)), d_rs=dma((2, 2, 4)),
+        vs=pltpu.VMEM((NB, W, NW), BF),
+        vs_ss=dma((NB,)), vs_rs=dma((NB,)),
     )
     for k in CHUNKS:
         r = SIZES[k]
@@ -77,12 +76,18 @@
             f"got{k}": pltpu.VMEM((3, HALVES[k], r, W // HALVES[k]), BF),
             f"raw_sem{k}": dma, f"a_ss{k}": dma((3, 2)), f"a_rs{k}": dma((3, 2)),
         })
-    for g in range(LAST + 1):
+    for g in range(len(GROUPS)):
         r = group_rows(g)
-        out[f"lhs{g}"] = pltpu.VMEM((2 * r, W), BF)
-        if g == LAST:
-            break
+        if g in DIRECT:
+            out.update({
+                f"part{g}": pltpu.VMEM((NB, r, NW), F32),
+                f"ds{g}": pltpu.VMEM((2, 4, r, NW), BF),
+                f"dr{g}": pltpu.VMEM((2, 4, r, NW), BF),
+                f"d_ss{g}": dma((2, 4)), f"d_rs{g}": dma((2, 4)),
+            })
+            continue
         out.update({
+            f"lhs{g}": pltpu.VMEM((2 * r, W), BF),
             f"pk{g}": pltpu.VMEM((2, 4, r, NW), F32),
             f"cs{g}": pltpu.VMEM((2, 4, r, NW), BF),
             f"cr{g}": pltpu.VMEM((2, 4, r, NW), BF),
@@ -155,8 +160,8 @@
     start_raw(0)
 
     barrier = pltpu.get_barrier_semaphore()
-    far = [dev(1 - xh, core, low, yy) for core in (0, 1) for low in (0, 1) for yy in range(4)]
-    for peer in far + [sibling, near] + y_peer:
+    far = [dev(1 - xh, c, low, yy) for low in (0, 1) for yy in range(4)]
+    for peer in far + [far_other, sibling, near] + y_peer:
         pl.semaphore_signal(barrier, inc=1, device_id=peer, device_id_type=MESH)
     for h in (0, 1):
         @pl.when(jnp.logical_not(jnp.logical_and(on_diag, here == h)))
@@ -174,7 +179,8 @@
 
     def a_copies(k):
         far_q = 2 * (1 - xh)
-        plan = ((far_q + c, far_same), (far_q + 1 - c, far_other), (2 * xh + 1 - c, sibling))
+        second = far_same if k in FROM_BOTH else far_other
+        plan = ((far_q + c, far_same), (far_q + 1 - c, second), (2 * xh + 1 - c, sibling))
         return [
             [
                 remote(
@@ -219,7 +225,7 @@
     for k in CHUNKS:
         spread(k)
         if k == 0:
-            pl.semaphore_wait(barrier, 23 - on_diag.astype(jnp.int32))
+            pl.semaphore_wait(barrier, 16 - on_diag.astype(jnp.int32))
         plan = a_copies(k)
         for cut in range(HALVES[k]):
             for n in range(3):
@@ -300,28 +306,56 @@
             m[f"cs{g}"][n // 4, n % 4] = got[r:].astype(BF)
             return 0
 
-        half = W // 2
-
-        def first_half(n, _):
-            m["part"][n] = matmul(lhs[:, :half], v[n, :half, :])
+        lax.fori_loop(0, NB, column, 0, unroll=1 if g == 0 else 2)
+        c_copy(g).start()
+
+    def vs_copy(n):
+        return remote(v.at[n], m["vs"].at[n], m["vs_ss"].at[n], m["vs_rs"].at[n], sibling)
+
+    def share_v(first):
+        def start(n, _):
+            vs_copy(first + n).start()
             return 0
 
-        def second_half(n, _):
-            got = m["part"][n] + matmul(lhs[:, half:], v[n, half:, :])
-            for a in range(2):
-                m["ds"][a, n // 4, n % 4] = got[a * r:(a + 1) * r].astype(BF)
+        lax.fori_loop(0, NB // 2, start, 0)
+
+    def wait_v():
+        def wait(n, _):
+            vs_copy(n).wait_recv()
             return 0
 
-        if g == LAST:
-            lax.fori_loop(0, NB, first_half, 0, unroll=2)
-            last = GROUPS[g][0]
-            for n in range(2):
-                a_copies(last)[n][1].wait_recv()
-            lhs[:, half:] = stack([m[f"got{last}"][n, 1] for n in range(2)])
-            lax.fori_loop(0, NB, second_half, 0, unroll=2)
-        else:
-            lax.fori_loop(0, NB, column, 0, unroll=1 if g == 0 else 2)
-        for copy in direct() if g == LAST else [c_copy(g)]:
+        lax.fori_loop(0, NB, wait, 0)
+
+    def d_copies(g):
+        return [
+            remote(
+                m[f"ds{g}"].at[(xl + b) % 2, (y + d) % 4], m[f"dr{g}"].at[b, d],
+                m[f"d_ss{g}"].at[b, d], m[f"d_rs{g}"].at[b, d],
+                dev(1 - xh, c, (xl + b) % 2, (y + d) % 4),
+            )
+            for b in range(2) for d in range(4)
+        ]
+
+    def multiply_whole(g):
+        k = GROUPS[g][0]
+        part, depth = m[f"part{g}"], W // HALVES[k]
+        steps = [(cut, n) for cut in range(HALVES[k]) for n in range(2)]
+        for at, (cut, n) in enumerate(steps):
+            a_copies(k)[n][cut].wait_recv()
+            weights = v if n == 0 else m["vs"]
+
+            def column(b, _):
+                got = matmul(m[f"got{k}"][n, cut], weights[b, cut * depth:(cut + 1) * depth, :])
+                if at > 0:
+                    got = got + part[b]
+                if at < len(steps) - 1:
+                    part[b] = got
+                else:
+                    m[f"ds{g}"][b // 4, b % 4] = got.astype(BF)
+                return 0
+
+            lax.fori_loop(0, NB, column, 0, unroll=2)
+        for copy in d_copies(g):
             copy.start()
 
     def over_cores(g):
@@ -348,16 +382,6 @@
         for copy in x_copies(g):
             copy.start()
 
-    def direct():
-        return [
-            remote(
-                m["ds"].at[a, (xl + b) % 2, (y + d) % 4], m["dr"].at[a, b, d],
-                m["d_ss"].at[a, b, d], m["d_rs"].at[a, b, d],
-                dev(1 - xh, (c + a) % 2, (xl + b) % 2, (y + d) % 4),
-            )
-            for a in range(2) for b in range(2) for d in range(4)
-        ]
-
     total = m["total"]
 
     def over_x(g):
@@ -367,10 +391,10 @@
             return
         first = STARTS[GROUPS[g][0]]
         rows = slice(first, first + group_rows(g))
-        if g == LAST:
-            for copy in direct():
+        if g in DIRECT:
+            for copy in d_copies(g):
                 copy.wait_recv()
-            terms = [m["dr"][a, b, d] for a in range(2) for b in range(2) for d in range(4)]
+            terms = [m[f"dr{g}"][b, d] for b in range(2) for d in range(4)]
         else:
             for copy in x_copies(g):
                 copy.wait_recv()
@@ -440,19 +464,20 @@
         ts[ROWS - 8:TR, :] = jnp.zeros((16, NW), BF)
 
     multiply(0)
+    share_v(0)
     matrices()
     over_cores(0)
     multiply(1)
+    share_v(NB // 2)
     over_cores(1)
     over_y(0)
     multiply(2)
     over_y(1)
     over_cores(2)
-    multiply(3)
-    over_cores(3)
+    wait_v()
+    multiply_whole(3)
     over_y(2)
-    multiply(4)
-    over_y(3)
+    multiply_whole(4)
     over_x(0)
     over_x(1)
     over_x(2)
@@ -468,11 +493,11 @@
         for copies in a_copies(k):
             for copy in copies:
                 copy.wait_send()
-    for g in range(LAST):
-        for copy in [c_copy(g)] + y_copies(g) + x_copies(g):
+    for g in range(len(GROUPS)):
+        for copy in d_copies(g) if g in DIRECT else [c_copy(g)] + y_copies(g) + x_copies(g):
             copy.wait_send()
-    for copy in direct():
-        copy.wait_send()
+    for n in range(NB):
+        vs_copy(n).wait_send()
     for p in range(len(PIECES)):
         t_wait(p)
 

time: 66.9 us -> 65.4 us (0.978)
  Pallas kernels: 65.1 us -> 63.6 us
    pallas_call x1, Pallas kernels: 65.1 us -> 63.6 us  [shards(): pl.pallas_call(kernel, out_shape=jax.ShapeDtypeStruct((rows_j, rows_i, NW...]
where the time goes in v3:
time: 65.4 us; the launch traced here: 65.2 us
  Pallas kernels  63.6 us (97%)
  local copies, waits for them, and re-layouts  1.56 us (2%)
    pallas_call x1, Pallas kernels, shards(): pl.pallas_call(kernel, out_shape=jax.ShapeDtypeStruct((rows_j, rows_i, NW...  63.6 us
    unnamed x1, local copies, waits for them, and re-layouts  1.56 us

profile of v3, /device:TPU:37, one launch (start us, length us, event | category | flops | bytes accessed | tf_op | source)
XLA Modules:
  0.0 65.2 jit_solution(2983606413746848650)
XLA Ops:
  0.0 63.6 %ladder.1 = bf16[10,20,256]{2,1,0:T(8,128)(2,1)} custom-call(bf16[200,16,4,128]{3,2,1,0:T(4,128)(2,1)} %bitcast.6, bf16[1,2048,2048]{2,1,0:T(8,128)(2,1)} %vint.1, s32[4,16,20]{2,1,0:T(8,128)} %bitcast.8, s32[1,16]{1,0:T(1,128)} %pi_in.1, s32[1,16]{1,0:T(1,128)} %bitcast.9, s32[1,16,16]{2,1,0:T(8,128)} %im_in.1), custom_call_target="tpu_custom_call" | custom-call | tf_op jit(solution)/shard_map/ladder/pallas_call | solution.py:518
  63.7 1.6 %copy.8 = bf16[20,10,256]{2,0,1:T(8,128)(2,1)} copy(bf16[20,10,256]{2,0,1:T(8,128)(2,1)} %bitcast.7) | data formatting | bytes 204800

commit v4 on v3

--- a/solution.py
+++ b/solution.py
@@ -9,7 +9,7 @@
 BF = jnp.bfloat16
 F32 = jnp.float32
 ROWS = 200
-SIZES = (16, 64, 64, 40, 16)
+SIZES = (16, 80, 48, 40, 16)
 HALVES = (1, 1, 1, 1, 2)
 STARTS = tuple(sum(SIZES[:k]) for k in range(len(SIZES)))
 CHUNKS = range(len(SIZES))
@@ -50,20 +50,15 @@
 def scratch():
     dma = pltpu.SemaphoreType.DMA
     out = dict(
-        tm=pltpu.VMEM((4, BL, 20), jnp.int32),
-        pi=pltpu.VMEM((1, BL), jnp.int32),
-        si=pltpu.VMEM((1, BL), jnp.int32),
-        im=pltpu.VMEM((1, BL, BL), jnp.int32),
         v=pltpu.VMEM((NB, W, NW), BF),
         kx=pltpu.VMEM((NB, BL, NW), F32),
         expand=pltpu.VMEM((BL, W), BF),
         turn=pltpu.VMEM((ROWS, 2 * TB), BF),
-        swap=pltpu.VMEM((NW, NW), BF),
         total=pltpu.VMEM((ROWS, NW), F32),
         final=pltpu.VMEM((NW // VB, ROWS, VB), F32),
         ts=pltpu.VMEM((TR, NW), BF),
         tr=pltpu.VMEM((2, TR, NW), BF),
-        small_sem=dma((4,)), v_sem=dma((NB,)),
+        v_sem=dma((NB,)),
         t_ss=dma((3,)), t_rs=dma((3, 2)), t_ls=dma((3,)),
         vs=pltpu.VMEM((NB, W, NW), BF),
         vs_ss=dma((NB,)), vs_rs=dma((NB,)),
@@ -106,7 +101,7 @@
 SCRATCH = scratch()
 
 
-def kernel(amp, vint, tm_in, pi_in, si_in, im_in, out, *refs):
+def kernel(amp, vint, tm, keep, out, *refs):
     m = dict(zip(SCRATCH, refs))
     occi, z, virt = lax.axis_index("occi"), lax.axis_index("occj"), lax.axis_index("virt")
     xh, c = occi // 2, occi % 2
@@ -131,13 +126,6 @@
             device_id=peer, device_id_type=MESH,
         )
 
-    smalls = [
-        (ref, m[name], m["small_sem"].at[n])
-        for n, (ref, name) in enumerate(
-            ((tm_in, "tm"), (pi_in, "pi"), (si_in, "si"), (im_in, "im"))
-        )
-    ]
-
     def start_raw(k):
         def start(t, _):
             pltpu.make_async_copy(
@@ -156,7 +144,6 @@
         v_copy(n).start()
         return 0
 
-    pltpu.make_async_copy(*smalls[0]).start()
     start_raw(0)
 
     barrier = pltpu.get_barrier_semaphore()
@@ -169,13 +156,10 @@
             pl.semaphore_signal(barrier, inc=1, device_id=turned[h], device_id_type=MESH)
 
     start_raw(1)
-    for args in smalls[1:]:
-        pltpu.make_async_copy(*args).start()
 
     expand = m["expand"]
     expand[...] = bits(lax.shift_right_logical(iota((BL, W), 1), 7) == iota((BL, W), 0))
-    pltpu.make_async_copy(*smalls[0]).wait()
-    marks = [m["tm"][q].astype(F32).astype(BF) for q in range(4)]
+    marks = [tm[q].astype(BF) for q in range(4)]
 
     def a_copies(k):
         far_q = 2 * (1 - xh)
@@ -236,13 +220,9 @@
             lax.fori_loop(0, NB, start_v, 0)
 
     v = m["v"]
-    for args in smalls[1:]:
-        pltpu.make_async_copy(*args).wait()
-    eye = iota((BL, BL), 0) == iota((BL, BL), 1)
-    own_label = jnp.sum(jnp.where(eye, m["pi"][...], 0), axis=1, keepdims=True)
-    keep = jnp.where(own_label == m["si"][...], m["im"][0], 0).astype(F32).astype(BF)
+    flags = keep[...].astype(BF)
     for n in range(NB):
-        m["kx"][n] = matmul(keep, expand[:, n * NW:(n + 1) * NW])
+        m["kx"][n] = matmul(flags, expand[:, n * NW:(n + 1) * NW])
 
     def mask_v(n, _):
         v_copy(n).wait()
@@ -422,9 +402,8 @@
     def t_mine(p):
         return jnp.logical_and(on_diag, here == PIECES[p][0])
 
-    def mirror(first, rows):
-        some = matmul(total[first:first + rows].astype(BF), m["swap"][...]).astype(BF)
-        ts[first:first + rows, :] = some
+    def ready(first, rows):
+        ts[first:first + rows, :] = total[first:first + rows].astype(BF)
 
     def t_start(p):
         @pl.when(t_mine(p))
@@ -459,8 +438,6 @@
         jt = rt - 10 * it
         ht = jnp.where(it >= 10, 1, 0)
         m["turn"][...] = bits(ct == TB * ht + 4 * here + jt * 10 + it - 10 * ht)
-        aw, bw = iota((NW, NW), 0), iota((NW, NW), 1)
-        m["swap"][...] = bits(aw == bw + 1 - 2 * jnp.bitwise_and(bw, 1))
         ts[ROWS - 8:TR, :] = jnp.zeros((16, NW), BF)
 
     multiply(0)
@@ -481,12 +458,12 @@
     over_x(0)
     over_x(1)
     over_x(2)
-    mirror(0, 144)
+    ready(0, 144)
     t_start(0)
     t_start(1)
     over_x(3)
     over_x(4)
-    mirror(144, 56)
+    ready(144, 56)
     t_start(2)
 
     for k in CHUNKS:
@@ -503,7 +480,10 @@
 
     rows = pl.ds(pl.multiple_of(TCUT * here, 16), TB)
     arrived = jnp.concatenate([tr[0, rows, :], tr[1, rows, :]], axis=0)
-    both = total[...] + matmul(m["turn"][...], arrived)
+    across = matmul(m["turn"][...], arrived)
+    odd = jnp.bitwise_and(iota((ROWS, NW), 1), 1) == 1
+    across = jnp.where(odd, pltpu.roll(across, 1, 1), pltpu.roll(across, NW - 1, 1))
+    both = total[...] + across
     for n in range(NW // VB):
         lanes = slice(n * VB, (n + 1) * VB)
         m["final"][n] = both[:, lanes]
@@ -515,19 +495,20 @@
     rows_i, rows_j, groups, _ = amplitude.shape
     tiles = amplitude.reshape(ROWS, groups, BL, VB).transpose(0, 2, 1, 3)
     hbm = pl.BlockSpec(memory_space=pltpu.HBM)
+    vmem = pl.BlockSpec(memory_space=pltpu.VMEM)
+    keep = (pair_irrep[0][:, None] == slice_irrep[None, :]) * integral_mask[0]
     result = pl.pallas_call(
         kernel,
         out_shape=jax.ShapeDtypeStruct((rows_j, rows_i, NW), BF),
-        in_specs=[hbm] * 6,
+        in_specs=[hbm, hbm, vmem, vmem],
         out_specs=pl.BlockSpec(memory_space=pltpu.VMEM),
         scratch_shapes=list(SCRATCH.values()),
         compiler_params=pltpu.CompilerParams(
-            collective_id=0, has_side_effects=True, vmem_limit_bytes=56 * 2**20
+            collective_id=0, has_side_effects=True, vmem_limit_bytes=52 * 2**20
         ),
         name="ladder",
     )(
-        tiles, integral, tile_mask.transpose(1, 2, 0), pair_irrep,
-        slice_irrep.reshape(1, -1), integral_mask,
+        tiles, integral, tile_mask.transpose(1, 2, 0).astype(F32), keep.astype(F32),
     )
     return result.transpose(1, 0, 2)
 

time: 65.4 us -> 65.6 us (level)
  other arithmetic: 0 us -> 1.55 us
  local copies, waits for them, and re-layouts: 1.56 us -> 0.65 us
    convert_element_type x0 -> x2, other arithmetic: none -> 1.55 us  [the longest x1 0.78 us: shards(): keep.astype(F32)]
    unnamed x1, local copies, waits for them, and re-layouts: 1.56 us -> 0.65 us
where the time goes in v4:
time: 65.6 us; the launch traced here: 65.3 us
  Pallas kernels  63.1 us (96%)
  other arithmetic  1.55 us (2%)
    pallas_call x1, Pallas kernels, shards(): pl.pallas_call(kernel, out_shape=jax.ShapeDtypeStruct((rows_j, rows_i, NW...  63.1 us

profile of v4, /device:TPU:37, one launch (start us, length us, event | category | flops | bytes accessed | tf_op | source)
XLA Modules:
  0.0 65.3 jit_solution(17853515238437099667)
XLA Ops:
  0.0 0.8 %fusion.keep = f32[16,16]{1,0:T(8,128)S(1)} fusion(s32[1,16,16]{2,1,0:T(8,128)} %param.11, s32[16]{0:T(128)} %param.10, s32[16]{0:T(128)} %bitcast.13), kind=kLoop, calls=%fused_computation.2 | loop fusion | flops 768 | bytes 2176 | tf_op jit(solution)/shard_map/convert_element_type | solution.py:511
  0.8 0.8 %convert_bitcast_fusion.tm = f32[4,16,20]{2,1,0:T(8,128)S(1)} fusion(s32[20,4,16]{0,2,1:T(8,128)} %param.8), kind=kLoop, calls=%fused_computation | loop fusion | flops 1280 | bytes 10240 | tf_op jit(solution)/shard_map/convert_element_type | solution.py:511
  1.5 63.1 %ladder.1 = bf16[10,20,256]{2,1,0:T(8,128)(2,1)S(1)} custom-call(bf16[200,16,4,128]{3,2,1,0:T(4,128)(2,1)} %bitcast.12, bf16[1,2048,2048]{2,1,0:T(8,128)(2,1)} %vint.1, f32[4,16,20]{2,1,0:T(8,128)S(1)} %convert_bitcast_fusion.tm, f32[16,16]{1,0:T(8,128)S(1)} %fusion.keep), custom_call_target="tpu_custom_call" | custom-call | tf_op jit(solution)/shard_map/ladder/pallas_call | solution.py:500
  64.7 0.7 copy.8

commit v5 on v4

--- a/solution.py
+++ b/solution.py
@@ -9,7 +9,7 @@
 BF = jnp.bfloat16
 F32 = jnp.float32
 ROWS = 200
-SIZES = (16, 80, 48, 40, 16)
+SIZES = (16, 64, 64, 40, 16)
 HALVES = (1, 1, 1, 1, 2)
 STARTS = tuple(sum(SIZES[:k]) for k in range(len(SIZES)))
 CHUNKS = range(len(SIZES))
@@ -459,8 +459,8 @@
     over_x(1)
     over_x(2)
     ready(0, 144)
+    t_start(1)
     t_start(0)
-    t_start(1)
     over_x(3)
     over_x(4)
     ready(144, 56)

time: 65.6 us -> 65.7 us (level)
  no operation moved by 1% of the time
where the time goes in v5:
time: 65.7 us; the launch traced here: 64.9 us
  Pallas kernels  62.7 us (95%)
  other arithmetic  1.55 us (2%)
    pallas_call x1, Pallas kernels, shards(): pl.pallas_call(kernel, out_shape=jax.ShapeDtypeStruct((rows_j, rows_i, NW...  62.7 us

profile of v5, /device:TPU:37, one launch (start us, length us, event | category | flops | bytes accessed | tf_op | source)
XLA Modules:
  0.0 64.9 jit_solution(5327507178464749371)
XLA Ops:
  0.0 0.8 %fusion.keep = f32[16,16]{1,0:T(8,128)S(1)} fusion(s32[1,16,16]{2,1,0:T(8,128)} %param.11, s32[16]{0:T(128)} %param.10, s32[16]{0:T(128)} %bitcast.13), kind=kLoop, calls=%fused_computation.2 | loop fusion | flops 768 | bytes 2176 | tf_op jit(solution)/shard_map/convert_element_type | solution.py:511
  0.8 0.8 %convert_bitcast_fusion.tm = f32[4,16,20]{2,1,0:T(8,128)S(1)} fusion(s32[20,4,16]{0,2,1:T(8,128)} %param.8), kind=kLoop, calls=%fused_computation | loop fusion | flops 1280 | bytes 10240 | tf_op jit(solution)/shard_map/convert_element_type | solution.py:511
  1.5 62.7 %ladder.1 = bf16[10,20,256]{2,1,0:T(8,128)(2,1)S(1)} custom-call(bf16[200,16,4,128]{3,2,1,0:T(4,128)(2,1)} %bitcast.12, bf16[1,2048,2048]{2,1,0:T(8,128)(2,1)} %vint.1, f32[4,16,20]{2,1,0:T(8,128)S(1)} %convert_bitcast_fusion.tm, f32[16,16]{1,0:T(8,128)S(1)} %fusion.keep), custom_call_target="tpu_custom_call" | custom-call | tf_op jit(solution)/shard_map/ladder/pallas_call | solution.py:500
  64.3 0.7 %copy.8 = bf16[20,10,256]{2,0,1:T(8,128)(2,1)} copy(bf16[20,10,256]{2,0,1:T(8,128)(2,1)S(1)} %bitcast.11) | data formatting | bytes 204800
